TPU v7x, 256 devices: a whole 4x4x8 slice. The times are simulated.
256 devices in a mesh: prow: 8 (over x, core), pcol: 32 (over z, y).
Axes of the slice: x: 4, y: 4, z: 8, core: 2. Of those that a mesh axis runs over, the one named last changes fastest.
Arguments:
- rhs: float32 [64, 65536], P(None, 'pcol'), may hold values from -6 to 6
- pivots: int32 [65536], P('pcol'), may hold values from 0 to 65535, as said below
- tile_of: int32 [256], replicated, may hold values from 0 to 255, as said below
- upper_rows: bfloat16 [3, 2048, 65536], P(None, 'prow', 'pcol'), may hold values from -0.125 to 0.125
- upper_inv: bfloat16 [3, 2048, 2048], P(None, 'pcol', 'prow'), may hold values from -0.125 to 0.125
- lower_rows: bfloat16 [3, 2048, 65536], P(None, 'prow', 'pcol'), may hold values from -0.125 to 0.125
- lower_inv: bfloat16 [3, 2048, 2048], P(None, 'prow', 'pcol'), may hold values from -0.125 to 0.125
- solved: float32 [64, 65536], P(None, 'pcol'), may hold values from -6 to 6
Outputs:
- forward: float32 [64, 65536], P(None, 'pcol')
- backward: float32 [64, 65536], P(None, 'pcol')
Inputs may be any that keep to these rules, and one draw needn't show every extreme that they name: pivots[p] lies in the same tile of 256 storage columns as p, and each column of a tile appears once. `tile_of`: storage tile d * 256 / 32 + l holds global tile l * 32 + c(d), c a permutation of the process columns.
All inputs are finite; a program needn't handle non-finite values.
Results may differ from a plain program's by a relative error of at most 0.015.
Values may be sent and summed in bfloat16 or wider, within the bound.
No kernel may reach another device: no remote copies, remote signals or barrier semaphores. Data moves between devices by JAX's collectives and lax.ppermute only.
A program may use at most 64 MiB of HBM per device.

v0:
```python
import jax
import jax.numpy as jnp
from jax import lax
from jax.sharding import PartitionSpec as P

NB = 2048
TILE = 256
STEPS = 3


def body(rhs, pivots, tile_of, upper_rows, upper_inv, lower_rows, lower_inv, solved):
    pcol_index = lax.axis_index("pcol")
    prow_index = lax.axis_index("prow")
    width_here = rhs.shape[1]
    tiles_here = width_here // TILE
    tiles_block = NB // TILE
    prow_rows = upper_rows.shape[1]
    count = rhs.shape[0]
    my_tiles = lax.dynamic_slice_in_dim(tile_of, pcol_index * tiles_here, tiles_here)
    my_blocks = my_tiles // tiles_block
    cell_blocks = jnp.repeat(my_blocks, TILE)

    def locate(step):
        match = my_blocks == step
        holds = jnp.any(match)
        tile_slot = jnp.argmax(match)
        block_place = my_tiles[tile_slot] % tiles_block
        return (holds, tile_slot, block_place)

    def write_block(field, block_full, step):
        holds, tile_slot, block_place = locate(step)
        piece = lax.dynamic_slice_in_dim(block_full, block_place * TILE, TILE, 1).astype(
            jnp.float32
        )
        written = lax.dynamic_update_slice_in_dim(field, piece, tile_slot * TILE, 1)
        return jnp.where(holds, written, field)

    state = jnp.take(rhs, pivots - pcol_index * width_here, axis=1)
    finished = []
    for step in range(STEPS):
        holds, tile_slot, block_place = locate(step)
        piece = lax.dynamic_slice_in_dim(state, tile_slot * TILE, TILE, 1)
        piece = jnp.where(holds, piece, 0.0)
        buffer = jnp.zeros((count, NB), jnp.float32)
        buffer = lax.dynamic_update_slice_in_dim(buffer, piece, block_place * TILE, 1)
        block_part = lax.psum_scatter(
            buffer.astype(jnp.bfloat16), "pcol", scatter_dimension=1, tiled=True
        )
        inverse_part = jnp.dot(block_part, upper_inv[step], preferred_element_type=jnp.float32)
        block_rows = lax.psum(inverse_part, "pcol").astype(jnp.bfloat16)
        block_full = lax.all_gather(block_rows, "prow", axis=1, tiled=True)
        update = jnp.dot(block_rows, upper_rows[step], preferred_element_type=jnp.float32)
        total = lax.psum(update, "prow")
        state = state - jnp.where(cell_blocks > step, total, 0.0)
        state = write_block(state, block_full, step)
        finished.append(block_full)
    solution = solved
    for step in reversed(range(STEPS)):
        known = jnp.where(cell_blocks > step, solution, 0.0).astype(jnp.bfloat16)
        partial_value = lax.dot_general(
            known, lower_rows[step], (((1,), (1,)), ((), ())), preferred_element_type=jnp.float32
        )
        sums = lax.psum(partial_value, "pcol")
        own_rows = lax.dynamic_slice_in_dim(
            finished[step], prow_index * prow_rows, prow_rows, 1
        ).astype(jnp.float32)
        resid = (own_rows - sums).astype(jnp.bfloat16)
        inverse_part = jnp.dot(resid, lower_inv[step], preferred_element_type=jnp.float32)
        new_cols = lax.psum(inverse_part, "prow").astype(jnp.bfloat16)
        new_block = lax.all_gather(new_cols, "pcol", axis=1, tiled=True)
        solution = write_block(solution, new_block, step)
    return (state, solution)


def solution(mesh):
    return jax.shard_map(
        body,
        mesh=mesh,
        in_specs=(
            P(None, "pcol"),
            P("pcol"),
            P(),
            P(None, "prow", "pcol"),
            P(None, "pcol", "prow"),
            P(None, "prow", "pcol"),
            P(None, "prow", "pcol"),
            P(None, "pcol"),
        ),
        out_specs=(P(None, "pcol"), P(None, "pcol")),
        check_vma=False,
    )
```

profile of v0, /device:TPU:8, one launch (start us, length us, event | category | flops | bytes accessed | tf_op | source)
XLA Modules:
  0.0 1755.8 jit_solution(12627563569382211011)
XLA Ops:
  7.2 1.0 copy.45
  8.3 0.8 broadcast_compare_fusion
  11.0 0.7 compare_reduce_fusion.4
  13.1 0.7 compare_reduce_fusion.2
  17.1 1.4 fusion.55
  20.4 0.7 fusion.51
  22.6 0.7 compare_reduce_fusion.1
  23.3 1.4 copy.12
  24.7 5.5 gather_fusion
  31.3 1.0 copy.20
  32.3 215.0 %reduce-scatter.10.cloned.1.call-done = bf16[64,64]{1,0:T(8,128)(2,1)} async-done(((bf16[2048,64]{1,0:T(8,128)(2,1)}), bf16[64,64]{1,0:T(8,128)(2,1)}) %reduce-scatter.10.cloned.1.call-update) | async-done | bytes 8208
  247.3 0.9 fusion.34
  248.2 136.2 %psum.84 = bf16[64,256]{1,0:T(8,128)(2,1)S(1)} all-reduce(f32[64,256]{1,0:T(8,128)S(1)} %fusion.34), channel_id=1, replica_groups=mesh['prow'=8,'pcol'=32] {'pcol'}, use_global_device_ids=true, to_apply=%region_3.4 | all-reduce | flops 16384 | bytes 98304 | tf_op jit(solution)/shard_map/psum | solution.py:50
  384.4 2.3 fusion.10
  389.3 13.2 all_gather.18
  402.5 52.6 %all-reduce.7.cloned.1.call-done = f32[64,2048]{1,0:T(8,128)} async-done(((f32[64,2048]{1,0:T(8,128)}), f32[64,2048]{1,0:T(8,128)}) %all-reduce.7.cloned.1.call-update) | async-done | bytes 524304 | tf_op jit(solution)/shard_map/psum | solution.py:53
  455.1 1.1 bitcast_subtract_fusion
  457.6 1.0 copy.22
  458.7 212.1 %reduce-scatter.12.cloned.1.call-done = bf16[64,64]{1,0:T(8,128)(2,1)} async-done(((bf16[2048,64]{1,0:T(8,128)(2,1)}), bf16[64,64]{1,0:T(8,128)(2,1)}) %reduce-scatter.12.cloned.1.call-update) | async-done | bytes 8208
  670.8 0.9 fusion.32
  671.7 136.1 %psum.86 = bf16[64,256]{1,0:T(8,128)(2,1)S(1)} all-reduce(f32[64,256]{1,0:T(8,128)S(1)} %fusion.32), channel_id=1, replica_groups=mesh['prow'=8,'pcol'=32] {'pcol'}, use_global_device_ids=true, to_apply=%region_8.9 | all-reduce | flops 16384 | bytes 98304 | tf_op jit(solution)/shard_map/psum | solution.py:50
  807.8 2.3 fusion.8
  812.6 13.1 all_gather.19
  825.8 52.8 %all-reduce.9.cloned.1.call-done = f32[64,2048]{1,0:T(8,128)} async-done(((f32[64,2048]{1,0:T(8,128)}), f32[64,2048]{1,0:T(8,128)}) %all-reduce.9.cloned.1.call-update) | async-done | bytes 524304 | tf_op jit(solution)/shard_map/psum | solution.py:53
  878.6 1.1 select_subtract_fusion.1
  879.7 0.7 select_dynamic-update-slice_fusion.5
  881.0 1.0 copy.24
  882.2 2.3 fusion.4
  884.6 209.7 %reduce-scatter.14.cloned.1.call-done = bf16[64,64]{1,0:T(8,128)(2,1)} async-done(((bf16[2048,64]{1,0:T(8,128)(2,1)}), bf16[64,64]{1,0:T(8,128)(2,1)}) %reduce-scatter.14.cloned.1.call-update) | async-done | bytes 8208
  1094.3 0.9 fusion.30
  1095.2 136.1 %psum.88 = bf16[64,256]{1,0:T(8,128)(2,1)S(1)} all-reduce(f32[64,256]{1,0:T(8,128)S(1)} %fusion.30), channel_id=1, replica_groups=mesh['prow'=8,'pcol'=32] {'pcol'}, use_global_device_ids=true, to_apply=%region_13.14 | all-reduce | flops 16384 | bytes 98304 | tf_op jit(solution)/shard_map/psum | solution.py:50
  1231.3 13.1 all_gather.20
  1244.5 1.0 fusion.24
  1245.4 25.8 %psum.91 = bf16[64,64]{1,0:T(8,128)(2,1)S(1)} all-reduce(f32[64,64]{1,0:T(8,128)S(1)} %fusion.24), channel_id=1, replica_groups=mesh['prow'=8,'pcol'=32] {'prow'}, use_global_device_ids=true, to_apply=%region_16.17 | all-reduce | flops 4096 | bytes 24576 | tf_op jit(solution)/shard_map/psum | solution.py:69
  1271.3 51.7 %all_gather.21 = bf16[64,2048]{0,1:T(8,128)(2,1)S(1)} all-gather(bf16[64,64]{0,1:T(8,128)(2,1)S(1)} %copy.14), channel_id=1, replica_groups=mesh['prow'=8,'pcol'=32] {'pcol'}, dimensions={1}, use_global_device_ids=true | all-gather | bytes 270336 | tf_op jit(solution)/shard_map/all_gather | solution.py:70
  1323.7 2.3 fusion.2
  1326.1 136.4 %all-reduce.15.cloned.1.call-done = f32[64,256]{1,0:T(8,128)} async-done(((f32[64,256]{1,0:T(8,128)}), f32[64,256]{1,0:T(8,128)}) %all-reduce.15.cloned.1.call-update) | async-done | bytes 65552 | tf_op jit(solution)/shard_map/psum | solution.py:63
  1462.5 1.0 fusion.25
  1463.4 23.6 %psum.93 = bf16[64,64]{1,0:T(8,128)(2,1)S(1)} all-reduce(f32[64,64]{1,0:T(8,128)S(1)} %fusion.25), channel_id=1, replica_groups=mesh['prow'=8,'pcol'=32] {'prow'}, use_global_device_ids=true, to_apply=%region_18.19 | all-reduce | flops 4096 | bytes 24576 | tf_op jit(solution)/shard_map/psum | solution.py:69
  1487.2 47.4 %all_gather.22 = bf16[64,2048]{0,1:T(8,128)(2,1)S(1)} all-gather(bf16[64,64]{0,1:T(8,128)(2,1)S(1)} %copy.16), channel_id=1, replica_groups=mesh['prow'=8,'pcol'=32] {'pcol'}, dimensions={1}, use_global_device_ids=true | all-gather | bytes 270336 | tf_op jit(solution)/shard_map/all_gather | solution.py:70
  1535.4 2.3 fusion
  1537.8 2.3 fusion.6
  1540.1 133.5 %all-reduce.17.cloned.1.call-done = f32[64,256]{1,0:T(8,128)} async-done(((f32[64,256]{1,0:T(8,128)}), f32[64,256]{1,0:T(8,128)}) %all-reduce.17.cloned.1.call-update) | async-done | bytes 65552 | tf_op jit(solution)/shard_map/psum | solution.py:63
  1673.7 1.0 fusion.26
  1674.6 23.6 %psum.95 = bf16[64,64]{1,0:T(8,128)(2,1)S(1)} all-reduce(f32[64,64]{1,0:T(8,128)S(1)} %fusion.26), channel_id=1, replica_groups=mesh['prow'=8,'pcol'=32] {'prow'}, use_global_device_ids=true, to_apply=%region_20.21 | all-reduce | flops 4096 | bytes 24576 | tf_op jit(solution)/shard_map/psum | solution.py:69
  1698.3 47.5 %all_gather.23 = bf16[64,2048]{0,1:T(8,128)(2,1)S(1)} all-gather(bf16[64,64]{0,1:T(8,128)(2,1)S(1)} %copy.18), channel_id=1, replica_groups=mesh['prow'=8,'pcol'=32] {'pcol'}, dimensions={1}, use_global_device_ids=true | all-gather | bytes 270336 | tf_op jit(solution)/shard_map/all_gather | solution.py:70
  1746.6 1.3 select_subtract_fusion
  1748.5 0.8 copy-done.1
  (57 shorter events, 8.3 us)
Async XLA Ops:
  7.2 240.1 %reduce-scatter.10.cloned.1.call-start = ((), (), s32[]{:S(2)}) async-start(), calls=%async_computation.9 | async-start | bytes 540672
  30.1 217.2 %copy-start.2 = (bf16[3,64,256]{2,1,0:T(8,128)(2,1)S(1)}, bf16[3,64,256]{2,1,0:T(8,128)(2,1)}, u32[]{:S(2)}) copy-start(bf16[3,64,256]{2,1,0:T(8,128)(2,1)} %param.12) | copy-start | bytes 294916
  32.3 422.8 %all-reduce.7.cloned.1.call-start = ((), (), s32[]{:S(2)}) async-start(), calls=%async_computation.3 | async-start | bytes 1048576 | tf_op jit(solution)/shard_map/psum | solution.py:53
  386.7 284.1 %reduce-scatter.12.cloned.1.call-start = ((), (), s32[]{:S(2)}) async-start(), calls=%async_computation.10 | async-start | bytes 540672
  458.7 419.9 %all-reduce.9.cloned.1.call-start = ((), (), s32[]{:S(2)}) async-start(), calls=%async_computation.4 | async-start | bytes 1048576 | tf_op jit(solution)/shard_map/psum | solution.py:53
  810.1 434.4 %copy-start.3 = (bf16[3,256,64]{1,2,0:T(8,128)(2,1)S(1)}, bf16[3,256,64]{1,2,0:T(8,128)(2,1)}, u32[]{:S(2)}) copy-start(bf16[3,256,64]{1,2,0:T(8,128)(2,1)} %param.14) | copy-start | bytes 294916
  810.1 284.2 %reduce-scatter.14.cloned.1.call-start = ((), (), s32[]{:S(2)}) async-start(), calls=%async_computation.11 | async-start | bytes 540672
  882.0 362.4 %all-reduce.13.cloned.1.call-start = ((), (), s32[]{:S(2)}) async-start(), calls=%async_computation.6 | async-start | bytes 131072 | tf_op jit(solution)/shard_map/psum | solution.py:63
  884.5 578.0 %all-reduce.15.cloned.1.call-start = ((), (), s32[]{:S(2)}) async-start(), calls=%async_computation.7 | async-start | bytes 131072 | tf_op jit(solution)/shard_map/psum | solution.py:63
  1326.1 347.6 %all-reduce.17.cloned.1.call-start = ((), (), s32[]{:S(2)}) async-start(), calls=%async_computation.8 | async-start | bytes 131072 | tf_op jit(solution)/shard_map/psum | solution.py:63
  1537.7 208.9 %all-reduce.11.cloned.1.call-start = ((), (), s32[]{:S(2)}) async-start(), calls=%async_computation.5 | async-start | bytes 1048576 | tf_op jit(solution)/shard_map/psum | solution.py:53
  1746.6 1.9 copy-start
  1748.5 0.8 copy-start.1
Sparse Core Ops, SparseCore 0:
  32.4 214.8 reduce-scatter.9
  386.8 68.2 all-reduce.6
  459.5 211.2 reduce-scatter.11
  810.3 68.2 all-reduce.8
  882.8 211.4 reduce-scatter.13
  1098.6 138.1 all-reduce.12
  1326.2 136.2 all-reduce.14
  1537.8 135.7 all-reduce.16
  1676.7 64.1 all-reduce.10
where the time goes:
time: 1760 us
  waiting for transfers between devices  1010 us (57%)
  blocking collectives  667 us (38%)
  between operations  27.6 us (2%)
  matrix products  19.4 us (1%)
    unnamed x12, waiting for transfers between devices  637 us
    psum x3, blocking collectives, body(): block_rows = lax.psum(inverse_part, 'pcol').astype(jnp.bfloat16)  408 us
    psum x3, waiting for transfers between devices, body(): sums = lax.psum(partial_value, 'pcol')  270 us
    all_gather x3, blocking collectives, body(): new_block = lax.all_gather(new_cols, 'pcol', axis=1, tiled=True)  147 us
    psum x3, waiting for transfers between devices, body(): total = lax.psum(update, 'prow')  105 us
    psum x3, blocking collectives, body(): new_cols = lax.psum(inverse_part, 'prow').astype(jnp.bfloat16)  73 us
    all_gather x3, blocking collectives, body(): block_full = lax.all_gather(block_rows, 'prow', axis=1, tiled=True)  39.4 us
  transfers between devices with their start and end apart: 9, of which 7 were waited for; matrix products, arithmetic and copies ran while one was open for 0% of the time, Pallas kernels for 0%

commit v1 on v0

--- a/solution.py
+++ b/solution.py
@@ -48,7 +48,26 @@
         )
         inverse_part = jnp.dot(block_part, upper_inv[step], preferred_element_type=jnp.float32)
         block_rows = lax.psum(inverse_part, "pcol").astype(jnp.bfloat16)
-        block_full = lax.all_gather(block_rows, "prow", axis=1, tiled=True)
+        peers, here, span = (lax.axis_size("prow"), lax.axis_index("prow"), block_rows.shape[1])
+        forward = [(i, (i + 1) % peers) for i in range(peers)]
+        backward = [(i, (i - 1) % peers) for i in range(peers)]
+        whole = jnp.zeros(
+            (*block_rows.shape[:1], peers * span, *block_rows.shape[1 + 1 :]), block_rows.dtype
+        )
+        whole = lax.dynamic_update_slice_in_dim(whole, block_rows, here * span, axis=1)
+        from_left = from_right = block_rows
+        halfway = peers // 2
+        for hop in range(1, halfway + 1):
+            from_left = lax.ppermute(from_left, "prow", forward)
+            whole = lax.dynamic_update_slice_in_dim(
+                whole, from_left, (here - hop) % peers * span, axis=1
+            )
+            if hop < peers - halfway:
+                from_right = lax.ppermute(from_right, "prow", backward)
+                whole = lax.dynamic_update_slice_in_dim(
+                    whole, from_right, (here + hop) % peers * span, axis=1
+                )
+        block_full = whole
         update = jnp.dot(block_rows, upper_rows[step], preferred_element_type=jnp.float32)
         total = lax.psum(update, "prow")
         state = state - jnp.where(cell_blocks > step, total, 0.0)

time: 1760 us -> 1760 us (level)
  blocking collectives: 667 us -> 626 us
  starting transfers between devices: 0.37 us -> 27 us
  waiting for transfers between devices: 1010 us -> 1030 us
    all_gather x3 -> x0, blocking collectives: 39.4 us -> none  [body(): block_full = lax.all_gather(block_rows, 'prow', axis=1, tiled=True)]
    ppermute x0 -> x21, starting transfers between devices: none -> 26.6 us  [the longest x9 26.5 us: body(): from_right = lax.ppermute(from_right, 'prow', backward)]
    ppermute x0 -> x21, waiting for transfers between devices: none -> 26.2 us  [the longest x12 26.1 us: body(): from_left = lax.ppermute(from_left, 'prow', forward)]
  transfers between devices with their start and end apart: 9 -> 30, of which waited for: 7 -> 18; matrix products, arithmetic and copies ran while one was open for 0% -> 1% of each run, Pallas kernels for 0% -> 0%
where the time goes in v1:
time: 1760 us
  waiting for transfers between devices  1030 us (59%)
  blocking collectives  626 us (36%)
  between operations  28.2 us (2%)
  starting transfers between devices  27 us (2%)
  matrix products  19.4 us (1%)
    unnamed x12, waiting for transfers between devices  632 us
    psum x3, blocking collectives, body(): block_rows = lax.psum(inverse_part, 'pcol').astype(jnp.bfloat16)  408 us
    psum x3, waiting for transfers between devices, body(): sums = lax.psum(partial_value, 'pcol')  268 us
    all_gather x3, blocking collectives, body(): new_block = lax.all_gather(new_cols, 'pcol', axis=1, tiled=True)  147 us
    psum x3, waiting for transfers between devices, body(): total = lax.psum(update, 'prow')  105 us
    psum x3, blocking collectives, body(): new_cols = lax.psum(inverse_part, 'prow').astype(jnp.bfloat16)  70.8 us
  transfers between devices with their start and end apart: 30, of which 18 were waited for; matrix products, arithmetic and copies ran while one was open for 1% of the time, Pallas kernels for 0%

profile of v1, /device:TPU:8, one launch (start us, length us, event | category | flops | bytes accessed | tf_op | source)
XLA Modules:
  0.0 1760.0 jit_solution(9111569378107520392)
XLA Ops:
  17.2 1.5 fusion.55
  23.4 1.4 copy.12
  24.8 5.5 gather_fusion
  35.0 212.3 %reduce-scatter.10.cloned.1.call-done = bf16[64,64]{1,0:T(8,128)(2,1)} async-done(((bf16[2048,64]{1,0:T(8,128)(2,1)}), bf16[64,64]{1,0:T(8,128)(2,1)}) %reduce-scatter.10.cloned.1.call-update) | async-done | bytes 8208
  248.3 136.2 %psum.84 = bf16[64,256]{1,0:T(8,128)(2,1)S(1)} all-reduce(f32[64,256]{1,0:T(8,128)S(1)} %fusion.34), channel_id=1, replica_groups=mesh['prow'=8,'pcol'=32] {'pcol'}, use_global_device_ids=true, to_apply=%region_3.4 | all-reduce | flops 16384 | bytes 98304 | tf_op jit(solution)/shard_map/psum | solution.py:50
  384.4 3.0 collective-permute-start.1
  387.4 2.3 fusion.10
  389.9 2.9 collective-permute-start.3
  392.8 1.6 collective-permute-done.2
  394.4 3.0 collective-permute-start.5
  397.4 1.6 collective-permute-done.4
  399.0 4.5 collective-permute-done.6
  403.5 53.4 %all-reduce.7.cloned.1.call-done = f32[64,2048]{1,0:T(8,128)} async-done(((f32[64,2048]{1,0:T(8,128)}), f32[64,2048]{1,0:T(8,128)}) %all-reduce.7.cloned.1.call-update) | async-done | bytes 524304 | tf_op jit(solution)/shard_map/psum | solution.py:72
  456.9 1.1 bitcast_subtract_fusion
  463.1 209.5 %reduce-scatter.12.cloned.1.call-done = bf16[64,64]{1,0:T(8,128)(2,1)} async-done(((bf16[2048,64]{1,0:T(8,128)(2,1)}), bf16[64,64]{1,0:T(8,128)(2,1)}) %reduce-scatter.12.cloned.1.call-update) | async-done | bytes 8208
  673.5 136.1 %psum.86 = bf16[64,256]{1,0:T(8,128)(2,1)S(1)} all-reduce(f32[64,256]{1,0:T(8,128)S(1)} %fusion.32), channel_id=1, replica_groups=mesh['prow'=8,'pcol'=32] {'pcol'}, use_global_device_ids=true, to_apply=%region_8.9 | all-reduce | flops 16384 | bytes 98304 | tf_op jit(solution)/shard_map/psum | solution.py:50
  809.6 2.3 fusion.8
  811.9 3.0 collective-permute-start.8
  815.0 1.5 collective-permute-done.7
  816.5 2.9 collective-permute-start.10
  819.5 1.6 collective-permute-done.9
  821.0 2.9 collective-permute-start.12
  824.0 1.6 collective-permute-done.11
  825.6 4.6 collective-permute-done.13
  830.2 51.8 %all-reduce.9.cloned.1.call-done = f32[64,2048]{1,0:T(8,128)} async-done(((f32[64,2048]{1,0:T(8,128)}), f32[64,2048]{1,0:T(8,128)}) %all-reduce.9.cloned.1.call-update) | async-done | bytes 524304 | tf_op jit(solution)/shard_map/psum | solution.py:72
  882.1 1.1 select_subtract_fusion.1
  885.6 2.3 fusion.4
  888.0 209.8 %reduce-scatter.14.cloned.1.call-done = bf16[64,64]{1,0:T(8,128)(2,1)} async-done(((bf16[2048,64]{1,0:T(8,128)(2,1)}), bf16[64,64]{1,0:T(8,128)(2,1)}) %reduce-scatter.14.cloned.1.call-update) | async-done | bytes 8208
  1098.7 136.1 %psum.88 = bf16[64,256]{1,0:T(8,128)(2,1)S(1)} all-reduce(f32[64,256]{1,0:T(8,128)S(1)} %fusion.30), channel_id=1, replica_groups=mesh['prow'=8,'pcol'=32] {'pcol'}, use_global_device_ids=true, to_apply=%region_13.14 | all-reduce | flops 16384 | bytes 98304 | tf_op jit(solution)/shard_map/psum | solution.py:50
  1234.8 3.0 collective-permute-start.15
  1237.8 1.6 collective-permute-done.14
  1239.4 2.9 collective-permute-start.17
  1242.3 1.6 collective-permute-done.16
  1243.9 2.9 collective-permute-start.19
  1246.9 1.6 collective-permute-done.18
  1248.5 4.5 collective-permute-done.20
  1254.0 23.6 %psum.91 = bf16[64,64]{1,0:T(8,128)(2,1)S(1)} all-reduce(f32[64,64]{1,0:T(8,128)S(1)} %fusion.24), channel_id=1, replica_groups=mesh['prow'=8,'pcol'=32] {'prow'}, use_global_device_ids=true, to_apply=%region_16.17 | all-reduce | flops 4096 | bytes 24576 | tf_op jit(solution)/shard_map/psum | solution.py:88
  1277.7 51.7 %all_gather.9 = bf16[64,2048]{0,1:T(8,128)(2,1)S(1)} all-gather(bf16[64,64]{0,1:T(8,128)(2,1)S(1)} %copy.14), channel_id=1, replica_groups=mesh['prow'=8,'pcol'=32] {'pcol'}, dimensions={1}, use_global_device_ids=true | all-gather | bytes 270336 | tf_op jit(solution)/shard_map/all_gather | solution.py:89
  1330.2 2.3 fusion.2
  1332.6 2.3 fusion.6
  1335.0 133.9 %all-reduce.15.cloned.1.call-done = f32[64,256]{1,0:T(8,128)} async-done(((f32[64,256]{1,0:T(8,128)}), f32[64,256]{1,0:T(8,128)}) %all-reduce.15.cloned.1.call-update) | async-done | bytes 65552 | tf_op jit(solution)/shard_map/psum | solution.py:82
  1469.8 23.6 %psum.93 = bf16[64,64]{1,0:T(8,128)(2,1)S(1)} all-reduce(f32[64,64]{1,0:T(8,128)S(1)} %fusion.25), channel_id=1, replica_groups=mesh['prow'=8,'pcol'=32] {'prow'}, use_global_device_ids=true, to_apply=%region_18.19 | all-reduce | flops 4096 | bytes 24576 | tf_op jit(solution)/shard_map/psum | solution.py:88
  1493.5 47.5 %all_gather.10 = bf16[64,2048]{0,1:T(8,128)(2,1)S(1)} all-gather(bf16[64,64]{0,1:T(8,128)(2,1)S(1)} %copy.16), channel_id=1, replica_groups=mesh['prow'=8,'pcol'=32] {'pcol'}, dimensions={1}, use_global_device_ids=true | all-gather | bytes 270336 | tf_op jit(solution)/shard_map/all_gather | solution.py:89
  1541.7 2.3 fusion
  1544.0 1.1 select_subtract_fusion
  1545.8 134.0 %all-reduce.17.cloned.1.call-done = f32[64,256]{1,0:T(8,128)} async-done(((f32[64,256]{1,0:T(8,128)}), f32[64,256]{1,0:T(8,128)}) %all-reduce.17.cloned.1.call-update) | async-done | bytes 65552 | tf_op jit(solution)/shard_map/psum | solution.py:82
  1680.8 23.6 %psum.95 = bf16[64,64]{1,0:T(8,128)(2,1)S(1)} all-reduce(f32[64,64]{1,0:T(8,128)S(1)} %fusion.26), channel_id=1, replica_groups=mesh['prow'=8,'pcol'=32] {'prow'}, use_global_device_ids=true, to_apply=%region_20.21 | all-reduce | flops 4096 | bytes 24576 | tf_op jit(solution)/shard_map/psum | solution.py:88
  1704.5 47.4 %all_gather.11 = bf16[64,2048]{0,1:T(8,128)(2,1)S(1)} all-gather(bf16[64,64]{0,1:T(8,128)(2,1)S(1)} %copy.18), channel_id=1, replica_groups=mesh['prow'=8,'pcol'=32] {'pcol'}, dimensions={1}, use_global_device_ids=true | all-gather | bytes 270336 | tf_op jit(solution)/shard_map/all_gather | solution.py:89
  (123 shorter events, 23.0 us)
Async XLA Ops:
  7.2 240.2 %reduce-scatter.10.cloned.1.call-start = ((), (), s32[]{:S(2)}) async-start(), calls=%async_computation.9 | async-start | bytes 540672
  30.3 217.1 %copy-start.2 = (bf16[3,64,256]{2,1,0:T(8,128)(2,1)S(1)}, bf16[3,64,256]{2,1,0:T(8,128)(2,1)}, u32[]{:S(2)}) copy-start(bf16[3,64,256]{2,1,0:T(8,128)(2,1)} %param.12) | copy-start | bytes 294916
  32.3 424.5 %all-reduce.7.cloned.1.call-start = ((), (), s32[]{:S(2)}) async-start(), calls=%async_computation.3 | async-start | bytes 1048576 | tf_op jit(solution)/shard_map/psum | solution.py:72
  384.4 5.4 collective-permute-start
  384.4 5.4 collective-permute-start.1
  389.7 282.9 %reduce-scatter.12.cloned.1.call-start = ((), (), s32[]{:S(2)}) async-start(), calls=%async_computation.10 | async-start | bytes 540672
  389.8 4.6 collective-permute-start.2
  389.9 4.5 collective-permute-start.3
  394.4 4.6 collective-permute-start.4
  394.4 4.6 collective-permute-start.5
  398.9 4.6 collective-permute-start.6
  460.3 421.8 %all-reduce.9.cloned.1.call-start = ((), (), s32[]{:S(2)}) async-start(), calls=%async_computation.4 | async-start | bytes 1048576 | tf_op jit(solution)/shard_map/psum | solution.py:72
  811.9 4.6 collective-permute-start.7
  811.9 4.6 collective-permute-start.8
  814.9 282.9 %reduce-scatter.14.cloned.1.call-start = ((), (), s32[]{:S(2)}) async-start(), calls=%async_computation.11 | async-start | bytes 540672
  816.5 4.6 collective-permute-start.9
  816.5 4.5 collective-permute-start.10
  821.0 4.6 collective-permute-start.11
  821.0 4.5 collective-permute-start.12
  824.0 429.0 %copy-start.3 = (bf16[3,256,64]{1,2,0:T(8,128)(2,1)S(1)}, bf16[3,256,64]{1,2,0:T(8,128)(2,1)}, u32[]{:S(2)}) copy-start(bf16[3,256,64]{1,2,0:T(8,128)(2,1)} %param.14) | copy-start | bytes 294916
  825.6 4.6 collective-permute-start.13
  885.5 367.6 %all-reduce.13.cloned.1.call-start = ((), (), s32[]{:S(2)}) async-start(), calls=%async_computation.6 | async-start | bytes 131072 | tf_op jit(solution)/shard_map/psum | solution.py:82
  887.9 580.9 %all-reduce.15.cloned.1.call-start = ((), (), s32[]{:S(2)}) async-start(), calls=%async_computation.7 | async-start | bytes 131072 | tf_op jit(solution)/shard_map/psum | solution.py:82
  1234.8 4.6 collective-permute-start.14
  1234.8 4.6 collective-permute-start.15
  1239.4 4.6 collective-permute-start.16
  1239.4 4.5 collective-permute-start.17
  1243.9 4.6 collective-permute-start.18
  1243.9 4.5 collective-permute-start.19
  1248.5 4.6 collective-permute-start.20
  1332.5 211.5 %all-reduce.11.cloned.1.call-start = ((), (), s32[]{:S(2)}) async-start(), calls=%async_computation.5 | async-start | bytes 1048576 | tf_op jit(solution)/shard_map/psum | solution.py:72
  1334.9 344.9 %all-reduce.17.cloned.1.call-start = ((), (), s32[]{:S(2)}) async-start(), calls=%async_computation.8 | async-start | bytes 131072 | tf_op jit(solution)/shard_map/psum | solution.py:82
  1545.8 206.9 %copy-start.1 = (f32[64,2048]{1,0:T(8,128)}, f32[64,2048]{1,0:T(8,128)S(1)}, u32[]{:S(2)}) copy-start(f32[64,2048]{1,0:T(8,128)S(1)} %select_dynamic-update-slice_fusion.3) | copy-start | bytes 1572868
  1752.7 0.8 copy-start
Sparse Core Ops, SparseCore 0:
  32.5 214.8 reduce-scatter.9
  389.8 67.0 all-reduce.6
  461.3 211.2 reduce-scatter.11
  815.0 67.0 all-reduce.8
  886.3 211.4 reduce-scatter.13
  1102.1 138.1 all-reduce.12
  1332.6 136.1 all-reduce.14
  1471.9 64.1 all-reduce.10
  1544.1 135.6 all-reduce.16
